TPU v7x, 32 devices: a whole 2x2x4 slice. The times are simulated.
32 devices in a mesh: px: 16 (over z, x, core), py: 2 (over y).
Axes of the slice: x: 2, y: 2, z: 4, core: 2. Of those that a mesh axis runs over, the one named last changes fastest.
Arguments:
- table: float32 [25, 50, 1000], replicated, may hold values from -1 to 1
- charge: float32 [64, 8, 8], P('px', 'py'), may hold values from 0.1 to 1
- hit_bins: int32 [64, 8, 8], P('px', 'py'), may hold values from 0 to 49
- hit_ticks: int32 [64, 8, 8], P('px', 'py'), may hold values from 0 to 23
- active: int32 [64, 8], P('px', 'py'), may hold values 0 or 1
- measured: bfloat16 [64, 8, 1024], P('px', 'py'), may hold values from -6 to 6
- row_module: int32 [64], replicated, may hold values from 0 to 6, as said below
- col_module: int32 [8], replicated, may hold values from 0 to 4, as said below
Outputs:
- current: bfloat16 [64, 8, 1024], P('px', 'py')
- table_grad: float32 [25, 50, 1000], P(None, None, 'py')
Inputs may be any that keep to these rules, and one draw needn't show every extreme that they name: `row_module`: starts at 0 and never falls; it rises by one at 6 rows. `col_module`: starts at 0 and never falls; it rises by one at 4 columns.
All inputs are finite; a program needn't handle non-finite values. No bound on the sum of `active` on one device may be relied on, other than what follows from the above.
Results may differ from a plain program's by a relative error of at most 0.014.
Values may be sent and summed in bfloat16 or wider, within the bound.
A program may use at most 128 MiB of HBM per device.

v0:
```python
import functools

import jax
import jax.numpy as jnp
from jax import lax
from jax.experimental import pallas as pl
from jax.experimental.pallas import tpu as pltpu
from jax.sharding import PartitionSpec as P

BINS = 50
SHIFTS = 24
REACH = 2
SPAN = 2 * REACH + 1
ROWS = 64
VMEM_BYTES = 48 * 1024 * 1024


def hot_rows(cc, hits, wide):
    bins = (lax.broadcasted_iota(jnp.int32, (ROWS, wide), 0) * SHIFTS).astype(jnp.float32)
    total = jnp.zeros((ROWS, wide), jnp.float32)
    for k in range(hits):
        code = jnp.broadcast_to(cc[k : k + 1], (ROWS, wide))
        load = jnp.broadcast_to(cc[hits + k : hits + k + 1], (ROWS, wide))
        total = jnp.where(code == bins, load, total)
    return total


def forward_kernel(hits, pixels, share, windows, cc_ref, table_ref, measured_ref, active_ref,
                   current_ref, window_ref, lhs, rhs):
    step = pl.program_id(0)
    wide = cc_ref.shape[2]
    ticks = table_ref.shape[2]
    wave = measured_ref.shape[1]
    for at in range(SPAN):
        hot = jnp.concatenate(
            [hot_rows(cc_ref[at, :, c : c + 128], hits, 128) for c in range(0, wide, 128)], axis=1
        )
        row = pl.multiple_of(step * (SPAN * ROWS) + at * ROWS, ROWS)
        lhs[pl.ds(row, ROWS), :] = hot.astype(jnp.bfloat16)
        weights = jnp.pad(table_ref[at], ((0, ROWS - BINS), (0, wave - ticks)))
        rhs[pl.ds(row, ROWS), :] = weights.astype(jnp.bfloat16)

    @pl.when(step == SPAN - 1)
    def _():
        spread = lax.dot_general(
            lhs[...], rhs[...], (((0,), (0,)), ((), ())), preferred_element_type=jnp.float32
        )
        total = spread[:pixels]
        for s in range(1, SHIFTS):
            total = total + pltpu.roll(spread[s * pixels : (s + 1) * pixels], s, axis=1)
        current_ref[...] = total.astype(jnp.bfloat16)
        resid = (total - measured_ref[...].astype(jnp.float32)) * active_ref[...]
        resid = resid.astype(jnp.bfloat16).astype(jnp.float32)
        reach = window_ref.shape[2]
        longer = jnp.pad(resid, ((0, 0), (0, reach)))
        length = longer.shape[1]
        for t in range(windows):
            moved = longer if t == 0 else pltpu.roll(longer, length - t * share, axis=1)
            window_ref[t] = moved[:, :reach].astype(jnp.bfloat16)


def backward_kernel(hits, scale, cols_ref, cc_ref, mask_ref, resid_ref, out_ref, lhs, rhs, acc):
    step = pl.program_id(0)
    wide = cc_ref.shape[2]
    count = resid_ref.shape[1]
    ticks = rhs.shape[2]
    slot = lax.rem(step, REACH + 1)

    @pl.when(step == 0)
    def _():
        acc[...] = jnp.zeros_like(acc)

    hot = jnp.concatenate(
        [hot_rows(cc_ref[0, :, c : c + 128], hits, 128) for c in range(0, wide, 128)], axis=1
    )
    for at in range(SPAN):
        moved = hot if at == REACH else pltpu.roll(hot, (at - REACH) % wide, axis=1)
        lhs[slot, at * ROWS : (at + 1) * ROWS, :] = (moved * mask_ref[at : at + 1]).astype(jnp.bfloat16)
    resid = resid_ref[0]
    for s in range(SHIFTS):
        rhs[slot, s * count : (s + 1) * count, :] = resid[:, s : s + ticks]

    def add(j, left, right):
        acc[j + REACH] += jnp.dot(lhs[left], rhs[right], preferred_element_type=jnp.float32)

    add(0, slot, slot)
    for back in range(1, REACH + 1):
        other = lax.rem(step + (REACH + 1) - back, REACH + 1)
        before = jnp.maximum(step - back, 0)

        @pl.when((step >= back) & (cols_ref[step] == cols_ref[before]))
        def _():
            add(-back, slot, other)
            add(back, other, slot)

    @pl.when(step == pl.num_programs(0) - 1)
    def _():
        for i in range(SPAN):
            for j in range(SPAN):
                part = acc[j, i * ROWS : i * ROWS + BINS, :]
                out_ref[i * SPAN + j] = part[:, : out_ref.shape[2]] * scale


def first_of(charge, hit_bins, hit_ticks):
    code = hit_bins * SHIFTS + hit_ticks
    same = code[..., :, None] == code[..., None, :]
    total = jnp.sum(jnp.where(same, charge[..., None, :], 0.0), axis=-1)
    hits = code.shape[-1]
    earlier = jnp.tril(jnp.ones((hits, hits), jnp.bool_), -1)
    first = ~jnp.any(same & earlier, axis=-1)
    code = jnp.where(first, code, -1).astype(jnp.float32)
    return jnp.concatenate([code, total.astype(jnp.bfloat16).astype(jnp.float32)], axis=-1)


def along_ticks(codes, hits):
    lanes = jnp.broadcast_to(codes[:, :, None, :], codes.shape[:2] + (SHIFTS, codes.shape[2]))
    ticks = jnp.arange(SHIFTS, dtype=jnp.float32)[:, None]
    is_code = (jnp.arange(2 * hits) < hits)[:, None, None]
    lanes = jnp.where(is_code, lanes - ticks, lanes)
    return lanes.reshape(codes.shape[0], codes.shape[1], SHIFTS * codes.shape[2])


def on_device(table, charge, hit_bins, hit_ticks, active, measured, row_module, col_module):
    tile_x, tile_y, hits = charge.shape
    pixels = tile_x * tile_y
    ticks = table.shape[2]
    wave = measured.shape[2]
    over_x, over_y = lax.axis_size("px"), lax.axis_size("py")
    rows, cols = tile_x * over_x, tile_y * over_y
    share = ticks // over_y
    ticks_wide = -(-share // 128) * 128
    reach = ticks_wide + 128

    packed = first_of(charge, hit_bins, hit_ticks)
    held = lax.all_gather(packed, ("px", "py"))
    held = held.reshape(over_x, over_y, tile_x, tile_y, 2 * hits)
    plane = held.transpose(0, 2, 1, 3, 4).reshape(rows, cols, 2 * hits)

    row_start = lax.axis_index("px") * tile_x
    col_start = lax.axis_index("py") * tile_y
    near = lax.dynamic_slice(
        jnp.pad(plane, ((REACH, REACH), (REACH, REACH), (0, 0)), constant_values=-1.0),
        (row_start, col_start, 0),
        (tile_x + 2 * REACH, tile_y + 2 * REACH, 2 * hits),
    )
    rows_pad = jnp.pad(row_module, REACH, constant_values=-1)
    cols_pad = jnp.pad(col_module, REACH, constant_values=-1)
    rows_near = lax.dynamic_slice_in_dim(rows_pad, row_start, tile_x + 2 * REACH, 0)
    cols_near = lax.dynamic_slice_in_dim(cols_pad, col_start, tile_y + 2 * REACH, 0)
    pieces = []
    for i in range(-REACH, REACH + 1):
        for j in range(-REACH, REACH + 1):
            at_x, at_y = slice(REACH - i, REACH - i + tile_x), slice(REACH - j, REACH - j + tile_y)
            row_same = rows_near[at_x] == rows_near[REACH : REACH + tile_x]
            col_same = cols_near[at_y] == cols_near[REACH : REACH + tile_y]
            allowed = row_same[:, None] & col_same[None, :]
            pieces.append(jnp.where(allowed[..., None], near[at_x, at_y], -1.0))
    sources = jnp.stack(pieces, 0).reshape(SPAN * SPAN, pixels, 2 * hits).transpose(0, 2, 1)
    sources = along_ticks(sources, hits)

    current, window = pl.pallas_call(
        functools.partial(forward_kernel, hits, pixels, share, over_y),
        grid=(SPAN,),
        in_specs=[
            pl.BlockSpec((SPAN, 2 * hits, SHIFTS * pixels), lambda g: (g, 0, 0)),
            pl.BlockSpec((SPAN, BINS, ticks), lambda g: (g, 0, 0)),
            pl.BlockSpec((pixels, wave), lambda g: (0, 0)),
            pl.BlockSpec((pixels, 1), lambda g: (0, 0)),
        ],
        out_specs=[
            pl.BlockSpec((pixels, wave), lambda g: (0, 0)),
            pl.BlockSpec((over_y, pixels, reach), lambda g: (0, 0, 0)),
        ],
        out_shape=[
            jax.ShapeDtypeStruct((pixels, wave), jnp.bfloat16),
            jax.ShapeDtypeStruct((over_y, pixels, reach), jnp.bfloat16),
        ],
        scratch_shapes=[
            pltpu.VMEM((SPAN * SPAN * ROWS, SHIFTS * pixels), jnp.bfloat16),
            pltpu.VMEM((SPAN * SPAN * ROWS, wave), jnp.bfloat16),
        ],
        compiler_params=pltpu.CompilerParams(vmem_limit_bytes=VMEM_BYTES),
        name="forward",
    )(
        sources,
        table,
        measured.reshape(pixels, wave),
        active.astype(jnp.float32).reshape(pixels, 1),
    )

    by_y = lax.all_to_all(window, "py", 0, 0)
    everyone = lax.all_gather(by_y, "px")
    everyone = everyone.reshape(over_x, over_y, tile_x, tile_y, reach)
    everyone = everyone.transpose(1, 3, 0, 2, 4).reshape(cols, rows, reach)

    columns = along_ticks(plane.transpose(1, 2, 0), hits)
    source_row = [
        lax.slice_in_dim(rows_pad, REACH - i, REACH - i + rows) for i in range(-REACH, REACH + 1)
    ]
    row_mask = jnp.stack([(r == row_module).astype(jnp.float32) for r in source_row], 0)
    row_mask = jnp.tile(jnp.pad(row_mask, ((0, 8 - SPAN), (0, 0))), (1, SHIFTS))

    gradient = pl.pallas_call(
        functools.partial(backward_kernel, hits, 1.0 / pixels),
        grid_spec=pltpu.PrefetchScalarGridSpec(
            num_scalar_prefetch=1,
            grid=(cols,),
            in_specs=[
                pl.BlockSpec((1, 2 * hits, SHIFTS * rows), lambda y, c: (y, 0, 0)),
                pl.BlockSpec((8, SHIFTS * rows), lambda y, c: (0, 0)),
                pl.BlockSpec((1, rows, reach), lambda y, c: (y, 0, 0)),
            ],
            out_specs=pl.BlockSpec((SPAN * SPAN, BINS, share), lambda y, c: (0, 0, 0)),
            scratch_shapes=[
                pltpu.VMEM((REACH + 1, SPAN * ROWS, SHIFTS * rows), jnp.bfloat16),
                pltpu.VMEM((REACH + 1, SHIFTS * rows, ticks_wide), jnp.bfloat16),
                pltpu.VMEM((SPAN, SPAN * ROWS, ticks_wide), jnp.float32),
            ],
        ),
        out_shape=jax.ShapeDtypeStruct((SPAN * SPAN, BINS, share), jnp.float32),
        compiler_params=pltpu.CompilerParams(vmem_limit_bytes=VMEM_BYTES),
        name="backward",
    )(col_module, columns, row_mask, everyone)
    return current.reshape(tile_x, tile_y, wave), gradient


def solution(mesh):
    in_specs = (
        P(),
        P("px", "py", None),
        P("px", "py", None),
        P("px", "py", None),
        P("px", "py"),
        P("px", "py", None),
        P(),
        P(),
    )
    out_specs = (P("px", "py", None), P(None, None, "py"))
    return jax.shard_map(
        on_device, mesh=mesh, in_specs=in_specs, out_specs=out_specs, check_vma=False
    )
```

profile of v0, /device:TPU:0, one launch (start us, length us, event | category | flops | bytes accessed | tf_op | source)
XLA Modules:
  0.0 136.8 jit_solution(17858816711697304884)
XLA Ops:
  0.7 0.7 pad_dynamic-slice_fusion.25
  1.4 0.7 pad_dynamic-slice_fusion.26
  2.1 0.1 iota_compare_fusion
  2.2 0.7 multiply_add_fusion
  2.9 0.4 fusion.1
  3.4 0.9 fusion
  4.3 0.1 pad_maximum_fusion
  4.4 71.0 %all-gather = f32[128,4,16]{2,1,0:T(4,128)S(1)} all-gather(f32[4,4,16]{2,1,0:T(4,128)S(1)} %pad_maximum_fusion), channel_id=2, replica_groups=mesh['px'=16,'py'=2] {'px','py'}, dimensions={0}, use_global_device_ids=true | all-gather | bytes 33792 | tf_op jit(solution)/shard_map/all_gather | solution.py:135
  75.4 0.1 slice_compare_fusion
  75.5 0.1 broadcast_and_fusion
  75.6 0.1 fusion.2
  75.8 0.1 fusion.25
  75.9 0.1 fusion.24
  76.1 0.1 fusion.23
  76.2 0.1 fusion.22
  76.4 0.1 copy.23
  76.5 0.0 copy-start.1
  76.6 0.0 copy-start.2
  76.6 2.5 %broadcast_in_dim.315 = f32[25,16,24,16]{3,2,1,0:T(8,128)} broadcast(f32[25,16,16]{2,1,0:T(8,128)S(1)} %copy.23), dimensions={0,1,3} | broadcast | bytes 640000 | tf_op jit(solution)/shard_map/broadcast_in_dim | solution.py:116
  79.1 3.7 %broadcast_in_dim.316 = f32[25,16,384]{2,1,0:T(8,128)S(1)} reshape(f32[25,16,24,16]{3,2,1,0:T(8,128)} %broadcast_in_dim.315) | data formatting | bytes 1228800 | tf_op jit(solution)/shard_map/broadcast_in_dim | solution.py:116
  82.8 0.1 sub.27
  82.9 0.0 copy-done.1
  82.9 0.0 copy-done.2
  82.9 0.1 reshape.575.active_ref
  83.0 0.1 subtract_select_fusion.1.cc_ref
  83.1 0.0 copy-start.3
  83.1 7.3 %forward.1 = (bf16[16,1024]{1,0:T(8,128)(2,1)S(1)}, bf16[2,16,640]{2,1,0:T(8,128)(2,1)}) custom-call(f32[25,16,384]{2,1,0:T(8,128)S(1)} %subtract_select_fusion.1.cc_ref, f32[25,50,1000]{2,1,0:T(8,128)} %table_ref.1, bf16[16,1024]{1,0:T(8,128)(2,1)S(1)} %reshape.562.measured_ref, f32[16,1]{1,0:T(8,128)S(1)} %reshape.575.active_ref), custom_call_target="tpu_custom_call" | custom-call | tf_op jit(solution)/shard_map/forward/pallas_call | solution.py:161
  90.5 3.3 %all-to-all-start = ((bf16[2,16,640]{2,1,0:T(8,128)(2,1)}), bf16[2,16,640]{2,1,0:T(8,128)(2,1)S(1)}, u32[]{:S(2)}, u32[]{:S(2)}) async-start(bf16[2,16,640]{2,1,0:T(8,128)(2,1)} %get-tuple-element.5), calls=%async_computation | async-start | bytes 81920 | tf_op jit(solution)/shard_map/all_to_all | solution.py:191
  93.8 0.1 copy.25
  93.9 0.0 copy-start
  93.9 0.1 broadcast_in_dim.318
  94.0 0.4 broadcast_in_dim.319
  94.4 0.1 sub.31
  94.5 0.2 subtract_select_fusion.cc_ref
  94.7 0.0 copy-done.3
  94.7 0.1 fusion.29
  94.8 0.1 tile.10.mask_ref
  94.9 0.6 reshape.564
  95.5 2.2 %all-to-all-done = bf16[2,16,640]{2,1,0:T(8,128)(2,1)S(1)} async-done(((bf16[2,16,640]{2,1,0:T(8,128)(2,1)}), bf16[2,16,640]{2,1,0:T(8,128)(2,1)S(1)}, u32[]{:S(2)}, u32[]{:S(2)}) %all-to-all-start) | async-done | bytes 40992 | tf_op jit(solution)/shard_map/all_to_all | solution.py:191
  97.7 19.1 %all-gather.1 = bf16[32,16,640]{2,1,0:T(8,128)(2,1)S(1)} all-gather(bf16[2,16,640]{2,1,0:T(8,128)(2,1)S(1)} %all-to-all-done), channel_id=3, replica_groups=mesh['px'=16,'py'=2] {'px'}, dimensions={0}, use_global_device_ids=true | all-gather | bytes 696320 | tf_op jit(solution)/shard_map/all_gather | solution.py:192
  116.9 0.1 reshape.565
  117.0 0.3 copy.28
  117.3 0.1 reshape.566.resid_ref
  117.4 0.0 copy-done
  117.5 19.3 %backward.1 = f32[25,50,500]{2,1,0:T(8,128)} custom-call(s32[8]{0:T(128)S(1)} %copy-done, f32[8,16,1536]{2,1,0:T(8,128)S(1)} %subtract_select_fusion.cc_ref, f32[8,1536]{1,0:T(8,128)S(1)} %tile.10.mask_ref, bf16[8,64,640]{2,1,0:T(8,128)(2,1)S(1)} %reshape.566.resid_ref), custom_call_target="tpu_custom_call" | custom-call | tf_op jit(solution)/shard_map/backward/pallas_call | solution.py:203
  (38 shorter events, 0.2 us)
Async XLA Ops:
  76.5 6.3 %copy-start.1 = (bf16[4,4,1024]{2,1,0:T(4,128)(2,1)S(1)}, bf16[4,4,1024]{2,1,0:T(4,128)(2,1)}, u32[]{:S(2)}) copy-start(bf16[4,4,1024]{2,1,0:T(4,128)(2,1)} %param.13) | copy-start | bytes 98308
  76.6 6.3 %copy-start.2 = (s32[4,4]{1,0:T(4,128)S(1)}, s32[4,4]{1,0:T(4,128)}, u32[]{:S(2)}) copy-start(s32[4,4]{1,0:T(4,128)} %param.12) | copy-start | bytes 196
  83.1 11.5 %copy-start.3 = (s32[64]{0:T(128)S(1)}, s32[64]{0:T(128)}, u32[]{:S(2)}) copy-start(s32[64]{0:T(128)} %param.14) | copy-start | bytes 772
  90.5 7.2 %all-to-all-start = ((bf16[2,16,640]{2,1,0:T(8,128)(2,1)}), bf16[2,16,640]{2,1,0:T(8,128)(2,1)S(1)}, u32[]{:S(2)}, u32[]{:S(2)}) async-start(bf16[2,16,640]{2,1,0:T(8,128)(2,1)} %get-tuple-element.5), calls=%async_computation | async-start | bytes 81920 | tf_op jit(solution)/shard_map/all_to_all | solution.py:191
  93.9 23.6 %copy-start = (s32[8]{0:T(128)S(1)}, s32[8]{0:T(128)}, u32[]{:S(2)}) copy-start(s32[8]{0:T(128)} %cols_ref.1) | copy-start | bytes 100
where the time goes:
time: 137 us
  blocking collectives  90.2 us (66%)
  Pallas kernels  26.7 us (19%)
  local copies, waits for them, and re-layouts  10.1 us (7%)
  starting transfers between devices  3.27 us (2%)
  other arithmetic  3.24 us (2%)
  waiting for transfers between devices  2.23 us (2%)
    all_gather x1, blocking collectives, on_device(): held = lax.all_gather(packed, ('px', 'py'))  71 us
    pallas_call x1, Pallas kernels, on_device(): pl.pallas_call(functools.partial(backward_kernel, hits, 1.0 / pixels), gr...  19.3 us
    all_gather x1, blocking collectives, on_device(): everyone = lax.all_gather(by_y, 'px')  19.1 us
    pallas_call x1, Pallas kernels, on_device(): pl.pallas_call(functools.partial(forward_kernel, hits, pixels, share, ove...  7.35 us
    broadcast_in_dim x4, local copies, waits for them, and re-layouts, along_ticks(): jnp.broadcast_to(codes[:, :, None, :], codes.shape[:2] + (SHIFTS, codes.s...  6.71 us
    all_to_all x1, starting transfers between devices, on_device(): by_y = lax.all_to_all(window, 'py', 0, 0)  3.27 us
  transfers between devices with their start and end apart: 1, of which 1 were waited for; matrix products, arithmetic and copies ran while one was open for 1% of the time, Pallas kernels for 0%

commit v1 on v0

--- a/solution.py
+++ b/solution.py
@@ -15,28 +15,119 @@
 VMEM_BYTES = 48 * 1024 * 1024
 
 
-def hot_rows(cc, hits, wide):
-    bins = (lax.broadcasted_iota(jnp.int32, (ROWS, wide), 0) * SHIFTS).astype(jnp.float32)
-    total = jnp.zeros((ROWS, wide), jnp.float32)
+def hot_rows(cc, hits, first_tick):
+    lanes = cc.shape[1]
+    bins = (lax.broadcasted_iota(jnp.int32, (ROWS, lanes), 0) * SHIFTS).astype(jnp.float32)
+    total = jnp.zeros((ROWS, lanes), jnp.float32)
     for k in range(hits):
-        code = jnp.broadcast_to(cc[k : k + 1], (ROWS, wide))
-        load = jnp.broadcast_to(cc[hits + k : hits + k + 1], (ROWS, wide))
+        code = jnp.broadcast_to(cc[k : k + 1] - first_tick, (ROWS, lanes))
+        load = jnp.broadcast_to(cc[hits + k : hits + k + 1], (ROWS, lanes))
         total = jnp.where(code == bins, load, total)
     return total
+
+
+def gather_kernel(source_ref, out_ref, own_sem, send_sem, recv_sem, on_sem, pass_sem):
+    over_x, over_y = out_ref.shape[0], out_ref.shape[1]
+    me_x, me_y = lax.axis_index("px"), lax.axis_index("py")
+    core = lax.rem(me_x, 2)
+    beside = me_x + 1 - 2 * core
+    chips = (over_x // 2) * over_y
+    here = (me_x // 2) * over_y + me_y
+
+    def place(chip):
+        return (chip // over_y) * 2 + core, lax.rem(chip, over_y)
+
+    barrier = pltpu.get_barrier_semaphore()
+
+    @pl.loop(1, chips)
+    def _(d):
+        pl.semaphore_signal(barrier, inc=1, device_id=place(lax.rem(here + d, chips)),
+                            device_id_type=pl.DeviceIdType.MESH)
+
+    pl.semaphore_signal(barrier, inc=1, device_id=(beside, me_y),
+                        device_id_type=pl.DeviceIdType.MESH)
+    own = pltpu.make_async_copy(source_ref.at[lax.rem(me_y, source_ref.shape[0])],
+                                out_ref.at[me_x, me_y], own_sem)
+    own.start()
+    pl.semaphore_wait(barrier, chips)
+
+    def send(d):
+        x, y = place(lax.rem(here + d, chips))
+        return pltpu.make_async_remote_copy(
+            src_ref=source_ref.at[lax.rem(y, source_ref.shape[0])],
+            dst_ref=out_ref.at[me_x, me_y],
+            send_sem=send_sem.at[d],
+            recv_sem=recv_sem.at[d],
+            device_id=(x, y),
+            device_id_type=pl.DeviceIdType.MESH,
+        )
+
+    def hand_on(d, source):
+        x, y = place(lax.rem(here + chips - d, chips))
+        return pltpu.make_async_remote_copy(
+            src_ref=source,
+            dst_ref=out_ref.at[x, y],
+            send_sem=on_sem.at[d],
+            recv_sem=pass_sem.at[d],
+            device_id=(beside, me_y),
+            device_id_type=pl.DeviceIdType.MESH,
+        )
+
+    def arrived(d):
+        x, y = place(lax.rem(here + chips - d, chips))
+        return out_ref.at[x, y]
+
+    mine = source_ref.at[lax.rem(me_y, source_ref.shape[0])]
+
+    @pl.loop(1, chips)
+    def _(d):
+        send(d).start()
+
+    hand_on(0, mine).start()
+
+    @pl.loop(1, chips)
+    def _(d):
+        send(d).wait_recv()
+        hand_on(d, arrived(d)).start()
+
+    hand_on(0, mine).wait()
+
+    @pl.loop(1, chips)
+    def _(d):
+        send(d).wait_send()
+        hand_on(d, arrived(d)).wait()
+
+    own.wait()
+
+
+def everywhere(blocks, over_x, over_y, number, name):
+    chips = (over_x // 2) * over_y
+    return pl.pallas_call(
+        gather_kernel,
+        in_specs=[pl.BlockSpec(memory_space=pltpu.VMEM)],
+        out_specs=pl.BlockSpec(memory_space=pltpu.VMEM),
+        out_shape=jax.ShapeDtypeStruct((over_x, over_y) + blocks.shape[1:], blocks.dtype),
+        scratch_shapes=[pltpu.SemaphoreType.DMA] + [pltpu.SemaphoreType.DMA((chips,))] * 4,
+        compiler_params=pltpu.CompilerParams(
+            collective_id=number, has_side_effects=True, vmem_limit_bytes=VMEM_BYTES
+        ),
+        name=name,
+    )(blocks)
 
 
 def forward_kernel(hits, pixels, share, windows, cc_ref, table_ref, measured_ref, active_ref,
                    current_ref, window_ref, lhs, rhs):
     step = pl.program_id(0)
-    wide = cc_ref.shape[2]
+    lanes = cc_ref.shape[2]
+    wide = SHIFTS * pixels
     ticks = table_ref.shape[2]
     wave = measured_ref.shape[1]
     for at in range(SPAN):
-        hot = jnp.concatenate(
-            [hot_rows(cc_ref[at, :, c : c + 128], hits, 128) for c in range(0, wide, 128)], axis=1
-        )
+        cc = cc_ref[at]
         row = pl.multiple_of(step * (SPAN * ROWS) + at * ROWS, ROWS)
-        lhs[pl.ds(row, ROWS), :] = hot.astype(jnp.bfloat16)
+        for c in range(0, wide, lanes):
+            hot = hot_rows(cc, hits, float(c // pixels))
+            lhs[pl.ds(row, ROWS), c : c + lanes] = hot.astype(jnp.bfloat16)
         weights = jnp.pad(table_ref[at], ((0, ROWS - BINS), (0, wave - ticks)))
         rhs[pl.ds(row, ROWS), :] = weights.astype(jnp.bfloat16)
 
@@ -61,8 +152,9 @@
 
 def backward_kernel(hits, scale, cols_ref, cc_ref, mask_ref, resid_ref, out_ref, lhs, rhs, acc):
     step = pl.program_id(0)
-    wide = cc_ref.shape[2]
+    lanes = cc_ref.shape[2]
     count = resid_ref.shape[1]
+    wide = SHIFTS * count
     ticks = rhs.shape[2]
     slot = lax.rem(step, REACH + 1)
 
@@ -70,12 +162,14 @@
     def _():
         acc[...] = jnp.zeros_like(acc)
 
-    hot = jnp.concatenate(
-        [hot_rows(cc_ref[0, :, c : c + 128], hits, 128) for c in range(0, wide, 128)], axis=1
-    )
-    for at in range(SPAN):
-        moved = hot if at == REACH else pltpu.roll(hot, (at - REACH) % wide, axis=1)
-        lhs[slot, at * ROWS : (at + 1) * ROWS, :] = (moved * mask_ref[at : at + 1]).astype(jnp.bfloat16)
+    cc = cc_ref[0]
+    for c in range(0, wide, lanes):
+        hot = hot_rows(cc, hits, float(c // count))
+        for at in range(SPAN):
+            moved = hot if at == REACH else pltpu.roll(hot, (at - REACH) % lanes, axis=1)
+            lhs[slot, at * ROWS : (at + 1) * ROWS, c : c + lanes] = (
+                moved * mask_ref[at : at + 1]
+            ).astype(jnp.bfloat16)
     resid = resid_ref[0]
     for s in range(SHIFTS):
         rhs[slot, s * count : (s + 1) * count, :] = resid[:, s : s + ticks]
@@ -113,11 +207,13 @@
 
 
 def along_ticks(codes, hits):
-    lanes = jnp.broadcast_to(codes[:, :, None, :], codes.shape[:2] + (SHIFTS, codes.shape[2]))
-    ticks = jnp.arange(SHIFTS, dtype=jnp.float32)[:, None]
+    count = codes.shape[2]
+    ticks = max(1, 128 // count)
+    lanes = jnp.broadcast_to(codes[:, :, None, :], codes.shape[:2] + (ticks, count))
+    after = jnp.arange(ticks, dtype=jnp.float32)[:, None]
     is_code = (jnp.arange(2 * hits) < hits)[:, None, None]
-    lanes = jnp.where(is_code, lanes - ticks, lanes)
-    return lanes.reshape(codes.shape[0], codes.shape[1], SHIFTS * codes.shape[2])
+    lanes = jnp.where(is_code, lanes - after, lanes)
+    return lanes.reshape(codes.shape[0], codes.shape[1], ticks * count)
 
 
 def on_device(table, charge, hit_bins, hit_ticks, active, measured, row_module, col_module):
@@ -132,7 +228,7 @@
     reach = ticks_wide + 128
 
     packed = first_of(charge, hit_bins, hit_ticks)
-    held = lax.all_gather(packed, ("px", "py"))
+    held = everywhere(packed.reshape(1, -1, 128), over_x, over_y, 0, "deposits")
     held = held.reshape(over_x, over_y, tile_x, tile_y, 2 * hits)
     plane = held.transpose(0, 2, 1, 3, 4).reshape(rows, cols, 2 * hits)
 
@@ -162,7 +258,7 @@
         functools.partial(forward_kernel, hits, pixels, share, over_y),
         grid=(SPAN,),
         in_specs=[
-            pl.BlockSpec((SPAN, 2 * hits, SHIFTS * pixels), lambda g: (g, 0, 0)),
+            pl.BlockSpec((SPAN, 2 * hits, sources.shape[2]), lambda g: (g, 0, 0)),
             pl.BlockSpec((SPAN, BINS, ticks), lambda g: (g, 0, 0)),
             pl.BlockSpec((pixels, wave), lambda g: (0, 0)),
             pl.BlockSpec((pixels, 1), lambda g: (0, 0)),
@@ -188,8 +284,7 @@
         active.astype(jnp.float32).reshape(pixels, 1),
     )
 
-    by_y = lax.all_to_all(window, "py", 0, 0)
-    everyone = lax.all_gather(by_y, "px")
+    everyone = everywhere(window, over_x, over_y, 1, "residuals")
     everyone = everyone.reshape(over_x, over_y, tile_x, tile_y, reach)
     everyone = everyone.transpose(1, 3, 0, 2, 4).reshape(cols, rows, reach)
 
@@ -198,7 +293,7 @@
         lax.slice_in_dim(rows_pad, REACH - i, REACH - i + rows) for i in range(-REACH, REACH + 1)
     ]
     row_mask = jnp.stack([(r == row_module).astype(jnp.float32) for r in source_row], 0)
-    row_mask = jnp.tile(jnp.pad(row_mask, ((0, 8 - SPAN), (0, 0))), (1, SHIFTS))
+    row_mask = jnp.tile(jnp.pad(row_mask, ((0, 8 - SPAN), (0, 0))), (1, columns.shape[2] // rows))
 
     gradient = pl.pallas_call(
         functools.partial(backward_kernel, hits, 1.0 / pixels),
@@ -206,8 +301,8 @@
             num_scalar_prefetch=1,
             grid=(cols,),
             in_specs=[
-                pl.BlockSpec((1, 2 * hits, SHIFTS * rows), lambda y, c: (y, 0, 0)),
-                pl.BlockSpec((8, SHIFTS * rows), lambda y, c: (0, 0)),
+                pl.BlockSpec((1, 2 * hits, columns.shape[2]), lambda y, c: (y, 0, 0)),
+                pl.BlockSpec((8, columns.shape[2]), lambda y, c: (0, 0)),
                 pl.BlockSpec((1, rows, reach), lambda y, c: (y, 0, 0)),
             ],
             out_specs=pl.BlockSpec((SPAN * SPAN, BINS, share), lambda y, c: (0, 0, 0)),

time: 137 us -> 61 us (0.45)
  the two profiles are of different devices: /device:TPU:0 before, /device:TPU:15 now
where the time goes in v1:
time: 61 us; the launch traced here: 60.6 us
  Pallas kernels  47 us (77%)
  local copies, waits for them, and re-layouts  7.92 us (13%)
  other arithmetic  4.66 us (8%)
  between operations  1.01 us (2%)
    pallas_call x2, Pallas kernels, everywhere(): pl.pallas_call(gather_kernel, in_specs=[pl.BlockSpec(memory_space=pltpu.V...  23.5 us
    pallas_call x1, Pallas kernels, on_device(): pl.pallas_call(functools.partial(backward_kernel, hits, 1.0 / pixels), gr...  19.7 us
    pallas_call x1, Pallas kernels, on_device(): pl.pallas_call(functools.partial(forward_kernel, hits, pixels, share, ove...  3.73 us
    unnamed x28, local copies, waits for them, and re-layouts  2.7 us

profile of v1, /device:TPU:15, one launch (start us, length us, event | category | flops | bytes accessed | tf_op | source)
XLA Modules:
  0.0 60.6 jit_solution(4331718358910556897)
XLA Ops:
  0.7 0.7 %pad_dynamic-slice_fusion.26 = s32[8]{0:T(128)S(1)} fusion(s32[]{:T(128)S(6)} %select_n.102, s32[64]{0:T(128)} %param.14), kind=kLoop, calls=%fused_computation.121 | loop fusion | bytes 292 | tf_op jit(solution)/shard_map/dynamic_slice | solution.py:244
  1.4 0.7 %pad_dynamic-slice_fusion.25 = s32[8]{0:T(128)S(1)} fusion(s32[]{:T(128)S(6)} %select_n.103, s32[8]{0:T(128)} %cols_ref.1), kind=kLoop, calls=%fused_computation.118 | loop fusion | bytes 68 | tf_op jit(solution)/shard_map/dynamic_slice | solution.py:245
  2.1 0.1 iota_compare_fusion
  2.2 0.1 sub.31
  2.3 0.7 %convert_element_type.24 = f32[4,4]{1,0:T(4,128)S(1)} convert(s32[4,4]{1,0:T(4,128)} %param.12) | non-fusion elementwise | flops 16 | bytes 128 | tf_op jit(solution)/shard_map/convert_element_type | solution.py:284
  3.0 0.9 %fusion.29 = (f32[1,64]{1,0:T(1,128)S(1)}, f32[1,64]{1,0:T(1,128)S(1)}, f32[1,64]{1,0:T(1,128)S(1)}, f32[1,64]{1,0:T(1,128)S(1)}) fusion(s32[64]{0:T(128)} %param.14), kind=kLoop, calls=%fused_computation.109 | loop fusion | flops 512 | bytes 1280 | tf_op jit(solution)/shard_map/stack | solution.py:295
  3.9 0.1 slice_compare_fusion
  4.0 0.1 tile.10.mask_ref
  4.1 0.1 sub.27
  4.2 0.1 reshape.575.active_ref
  4.3 0.7 %multiply_add_fusion = s32[4,4,8]{2,1,0:T(4,128)S(1)} fusion(s32[4,4,8]{2,1,0:T(4,128)} %param.11, s32[4,4,8]{2,1,0:T(4,128)} %param.10), kind=kLoop, calls=%fused_computation.59 | loop fusion | flops 256 | bytes 1536 | tf_op jit(solution)/shard_map/add | solution.py:199
  5.0 0.4 fusion.1
  5.4 0.9 %fusion = bf16[4,4,8]{2,1,0:T(4,128)(2,1)S(1)} fusion(f32[4,4,8]{2,1,0:T(4,128)} %param.9, s32[4,4,8]{2,1,0:T(4,128)S(1)} %multiply_add_fusion), kind=kLoop, calls=%fused_computation.30 | loop fusion | flops 2944 | bytes 1280 | tf_op jit(solution)/shard_map/reduce_sum | solution.py:201
  6.3 0.1 pad_maximum_fusion
  6.4 0.1 reshape.563.source_ref
  6.5 0.1 broadcast_and_fusion
  6.6 9.4 %deposits.1 = f32[16,2,2,128]{3,2,1,0:T(2,128)S(1)} custom-call(f32[1,2,128]{2,1,0:T(2,128)S(1)} %reshape.563.source_ref), custom_call_target="tpu_custom_call" | custom-call | tf_op jit(solution)/shard_map/deposits/pallas_call | solution.py:105
  16.0 0.8 %reshape.566.measured_ref = bf16[16,1024]{1,0:T(8,128)(2,1)S(1)} reshape(bf16[4,4,1024]{2,1,0:T(4,128)(2,1)} %param.13) | data formatting | bytes 65536 | tf_op jit(solution)/shard_map/reshape | solution.py:283
  16.8 0.2 reshape.564
  17.1 0.1 fusion.22
  17.2 0.1 fusion.23
  17.3 0.1 fusion.24
  17.4 0.1 fusion.25
  17.5 0.1 fusion.2
  17.6 0.1 copy.20
  17.8 0.1 broadcast_in_dim.318
  17.8 0.1 broadcast_in_dim.319
  18.0 0.1 subtract_select_fusion.1.cc_ref
  18.3 0.1 copy.18
  18.4 0.2 broadcast_in_dim.315
  18.6 0.4 broadcast_in_dim.316
  19.1 0.1 subtract_select_fusion.cc_ref
  19.1 0.0 copy-start
  19.2 2.6 %copy-done = f32[25,50,1000]{2,1,0:T(8,128)S(1)} copy-done((f32[25,50,1000]{2,1,0:T(8,128)S(1)}, f32[25,50,1000]{2,1,0:T(8,128)}, u32[]{:S(2)}) %copy-start) | copy-done | bytes 5000024
  21.8 3.7 %forward.1 = (bf16[16,1024]{1,0:T(8,128)(2,1)S(1)}, bf16[2,16,640]{2,1,0:T(8,128)(2,1)S(1)}) custom-call(f32[25,16,128]{2,1,0:T(8,128)S(1)} %subtract_select_fusion.cc_ref, f32[25,50,1000]{2,1,0:T(8,128)S(1)} %copy-done, bf16[16,1024]{1,0:T(8,128)(2,1)S(1)} %reshape.566.measured_ref, f32[16,1]{1,0:T(8,128)S(1)} %reshape.575.active_ref), custom_call_target="tpu_custom_call" | custom-call | tf_op jit(solution)/shard_map/forward/pallas_call | solution.py:257
  25.5 0.0 copy-start.1
  25.5 0.6 %reshape.568 = bf16[4,4,1024]{2,1,0:T(4,128)(2,1)} reshape(bf16[16,1024]{1,0:T(8,128)(2,1)S(1)} %get-tuple-element.4) | data formatting | bytes 65536 | tf_op jit(solution)/shard_map/reshape | solution.py:319
  26.1 14.1 %residuals.1 = bf16[16,2,16,640]{3,2,1,0:T(8,128)(2,1)S(1)} custom-call(bf16[2,16,640]{2,1,0:T(8,128)(2,1)S(1)} %get-tuple-element.5.source_ref), custom_call_target="tpu_custom_call" | custom-call | tf_op jit(solution)/shard_map/residuals/pallas_call | solution.py:105
  40.3 0.2 reshape.569
  40.4 0.3 copy.23
  40.7 0.1 reshape.570.resid_ref
  40.8 0.0 copy-done.1
  40.9 19.7 %backward.1 = f32[25,50,500]{2,1,0:T(8,128)} custom-call(s32[8]{0:T(128)S(1)} %copy-done.1, f32[8,16,128]{2,1,0:T(8,128)S(1)} %subtract_select_fusion.1.cc_ref, f32[8,128]{1,0:T(8,128)S(1)} %tile.10.mask_ref, bf16[8,64,640]{2,1,0:T(8,128)(2,1)S(1)} %reshape.570.resid_ref), custom_call_target="tpu_custom_call" | custom-call | tf_op jit(solution)/shard_map/backward/pallas_call | solution.py:298
  (36 shorter events, 0.2 us)
Async XLA Ops:
  19.1 2.6 %copy-start = (f32[25,50,1000]{2,1,0:T(8,128)S(1)}, f32[25,50,1000]{2,1,0:T(8,128)}, u32[]{:S(2)}) copy-start(f32[25,50,1000]{2,1,0:T(8,128)} %table_ref.1) | copy-start | bytes 15000004
  25.5 15.3 %copy-start.1 = (s32[8]{0:T(128)S(1)}, s32[8]{0:T(128)}, u32[]{:S(2)}) copy-start(s32[8]{0:T(128)} %cols_ref.1) | copy-start | bytes 100

commit v2 on v1

--- a/solution.py
+++ b/solution.py
@@ -11,8 +11,9 @@
 SHIFTS = 24
 REACH = 2
 SPAN = 2 * REACH + 1
-ROWS = 64
-VMEM_BYTES = 48 * 1024 * 1024
+ROWS = 56
+STACK = -(-SPAN * ROWS // 16) * 16
+MIB = 1024 * 1024
 
 
 def hot_rows(cc, hits, first_tick):
@@ -26,6 +27,17 @@
     return total
 
 
+def merged(cc, hits):
+    code, load = cc[:hits], cc[hits:]
+    row = lax.broadcasted_iota(jnp.int32, code.shape, 0)
+    total, spent = load, jnp.zeros(code.shape, jnp.float32)
+    for d in range(1, hits):
+        same = code == pltpu.roll(code, d, axis=0)
+        total = total + jnp.where(same, pltpu.roll(load, d, axis=0), 0.0)
+        spent = jnp.where(same & (row >= d), 1.0, spent)
+    return jnp.concatenate([jnp.where(spent > 0.0, -1000.0, code), total], axis=0)
+
+
 def gather_kernel(source_ref, out_ref, own_sem, send_sem, recv_sem, on_sem, pass_sem):
     over_x, over_y = out_ref.shape[0], out_ref.shape[1]
     me_x, me_y = lax.axis_index("px"), lax.axis_index("py")
@@ -35,13 +47,22 @@
     here = (me_x // 2) * over_y + me_y
 
     def place(chip):
-        return (chip // over_y) * 2 + core, lax.rem(chip, over_y)
-
+        return lax.div(chip, over_y) * 2 + core, lax.rem(chip, over_y)
+
+    def after(d):
+        chip = here + d
+        return jnp.where(chip >= chips, chip - chips, chip)
+
+    def ahead(d):
+        chip = here - d
+        return jnp.where(chip < 0, chip + chips, chip)
+
+    unroll = chips - 1 if chips <= 16 else 1
     barrier = pltpu.get_barrier_semaphore()
 
-    @pl.loop(1, chips)
+    @pl.loop(1, chips, unroll=unroll)
     def _(d):
-        pl.semaphore_signal(barrier, inc=1, device_id=place(lax.rem(here + d, chips)),
+        pl.semaphore_signal(barrier, inc=1, device_id=place(after(d)),
                             device_id_type=pl.DeviceIdType.MESH)
 
     pl.semaphore_signal(barrier, inc=1, device_id=(beside, me_y),
@@ -52,7 +73,7 @@
     pl.semaphore_wait(barrier, chips)
 
     def send(d):
-        x, y = place(lax.rem(here + d, chips))
+        x, y = place(after(d))
         return pltpu.make_async_remote_copy(
             src_ref=source_ref.at[lax.rem(y, source_ref.shape[0])],
             dst_ref=out_ref.at[me_x, me_y],
@@ -63,7 +84,7 @@
         )
 
     def hand_on(d, source):
-        x, y = place(lax.rem(here + chips - d, chips))
+        x, y = place(ahead(d))
         return pltpu.make_async_remote_copy(
             src_ref=source,
             dst_ref=out_ref.at[x, y],
@@ -74,25 +95,25 @@
         )
 
     def arrived(d):
-        x, y = place(lax.rem(here + chips - d, chips))
+        x, y = place(ahead(d))
         return out_ref.at[x, y]
 
     mine = source_ref.at[lax.rem(me_y, source_ref.shape[0])]
 
-    @pl.loop(1, chips)
+    @pl.loop(1, chips, unroll=unroll)
     def _(d):
         send(d).start()
 
     hand_on(0, mine).start()
 
-    @pl.loop(1, chips)
+    @pl.loop(1, chips, unroll=unroll)
     def _(d):
         send(d).wait_recv()
         hand_on(d, arrived(d)).start()
 
     hand_on(0, mine).wait()
 
-    @pl.loop(1, chips)
+    @pl.loop(1, chips, unroll=unroll)
     def _(d):
         send(d).wait_send()
         hand_on(d, arrived(d)).wait()
@@ -100,7 +121,7 @@
     own.wait()
 
 
-def everywhere(blocks, over_x, over_y, number, name):
+def everywhere(blocks, over_x, over_y, number, room, name):
     chips = (over_x // 2) * over_y
     return pl.pallas_call(
         gather_kernel,
@@ -109,7 +130,7 @@
         out_shape=jax.ShapeDtypeStruct((over_x, over_y) + blocks.shape[1:], blocks.dtype),
         scratch_shapes=[pltpu.SemaphoreType.DMA] + [pltpu.SemaphoreType.DMA((chips,))] * 4,
         compiler_params=pltpu.CompilerParams(
-            collective_id=number, has_side_effects=True, vmem_limit_bytes=VMEM_BYTES
+            collective_id=number, has_side_effects=True, vmem_limit_bytes=room * MIB
         ),
         name=name,
     )(blocks)
@@ -122,14 +143,18 @@
     wide = SHIFTS * pixels
     ticks = table_ref.shape[2]
     wave = measured_ref.shape[1]
-    for at in range(SPAN):
-        cc = cc_ref[at]
-        row = pl.multiple_of(step * (SPAN * ROWS) + at * ROWS, ROWS)
-        for c in range(0, wide, lanes):
-            hot = hot_rows(cc, hits, float(c // pixels))
-            lhs[pl.ds(row, ROWS), c : c + lanes] = hot.astype(jnp.bfloat16)
-        weights = jnp.pad(table_ref[at], ((0, ROWS - BINS), (0, wave - ticks)))
-        rhs[pl.ds(row, ROWS), :] = weights.astype(jnp.bfloat16)
+    first = pl.multiple_of(step * STACK, STACK)
+    spare = STACK - SPAN * ROWS
+    ccs = [merged(cc_ref[at], hits) for at in range(SPAN)]
+    for c in range(0, wide, lanes):
+        hot = [hot_rows(cc, hits, float(c // pixels)) for cc in ccs]
+        hot = jnp.concatenate(hot + [jnp.zeros((spare, lanes), jnp.float32)], axis=0)
+        lhs[pl.ds(first, STACK), c : c + lanes] = hot.astype(jnp.bfloat16)
+    weights = [
+        jnp.pad(table_ref[at], ((0, ROWS - BINS), (0, wave - ticks))) for at in range(SPAN)
+    ]
+    weights = jnp.concatenate(weights + [jnp.zeros((spare, wave), jnp.float32)], axis=0)
+    rhs[pl.ds(first, STACK), :] = weights.astype(jnp.bfloat16)
 
     @pl.when(step == SPAN - 1)
     def _():
@@ -162,14 +187,17 @@
     def _():
         acc[...] = jnp.zeros_like(acc)
 
-    cc = cc_ref[0]
+    cc = merged(cc_ref[0], hits)
+    spare = jnp.zeros((STACK - SPAN * ROWS, lanes), jnp.float32)
     for c in range(0, wide, lanes):
         hot = hot_rows(cc, hits, float(c // count))
-        for at in range(SPAN):
-            moved = hot if at == REACH else pltpu.roll(hot, (at - REACH) % lanes, axis=1)
-            lhs[slot, at * ROWS : (at + 1) * ROWS, c : c + lanes] = (
-                moved * mask_ref[at : at + 1]
-            ).astype(jnp.bfloat16)
+        turned = [
+            (hot if at == REACH else pltpu.roll(hot, (at - REACH) % lanes, axis=1))
+            * mask_ref[at : at + 1]
+            for at in range(SPAN)
+        ]
+        stacked = jnp.concatenate(turned + [spare], axis=0)
+        lhs[slot, :, c : c + lanes] = stacked.astype(jnp.bfloat16)
     resid = resid_ref[0]
     for s in range(SHIFTS):
         rhs[slot, s * count : (s + 1) * count, :] = resid[:, s : s + ticks]
@@ -193,17 +221,6 @@
             for j in range(SPAN):
                 part = acc[j, i * ROWS : i * ROWS + BINS, :]
                 out_ref[i * SPAN + j] = part[:, : out_ref.shape[2]] * scale
-
-
-def first_of(charge, hit_bins, hit_ticks):
-    code = hit_bins * SHIFTS + hit_ticks
-    same = code[..., :, None] == code[..., None, :]
-    total = jnp.sum(jnp.where(same, charge[..., None, :], 0.0), axis=-1)
-    hits = code.shape[-1]
-    earlier = jnp.tril(jnp.ones((hits, hits), jnp.bool_), -1)
-    first = ~jnp.any(same & earlier, axis=-1)
-    code = jnp.where(first, code, -1).astype(jnp.float32)
-    return jnp.concatenate([code, total.astype(jnp.bfloat16).astype(jnp.float32)], axis=-1)
 
 
 def along_ticks(codes, hits):
@@ -227,30 +244,39 @@
     ticks_wide = -(-share // 128) * 128
     reach = ticks_wide + 128
 
-    packed = first_of(charge, hit_bins, hit_ticks)
-    held = everywhere(packed.reshape(1, -1, 128), over_x, over_y, 0, "deposits")
+    packed = jnp.concatenate(
+        [(hit_bins * SHIFTS + hit_ticks).astype(jnp.float32), charge], axis=-1
+    )
+    held = everywhere(packed.reshape(1, -1, 128), over_x, over_y, 0, 4, "deposits")
     held = held.reshape(over_x, over_y, tile_x, tile_y, 2 * hits)
     plane = held.transpose(0, 2, 1, 3, 4).reshape(rows, cols, 2 * hits)
 
     row_start = lax.axis_index("px") * tile_x
     col_start = lax.axis_index("py") * tile_y
+    modules = jnp.stack(
+        [
+            jnp.broadcast_to(row_module[:, None], (rows, cols)),
+            jnp.broadcast_to(col_module[None, :], (rows, cols)),
+        ],
+        axis=-1,
+    ).astype(jnp.float32)
     near = lax.dynamic_slice(
-        jnp.pad(plane, ((REACH, REACH), (REACH, REACH), (0, 0)), constant_values=-1.0),
+        jnp.pad(
+            jnp.concatenate([plane, modules], axis=-1),
+            ((REACH, REACH), (REACH, REACH), (0, 0)),
+            constant_values=-1.0,
+        ),
         (row_start, col_start, 0),
-        (tile_x + 2 * REACH, tile_y + 2 * REACH, 2 * hits),
-    )
-    rows_pad = jnp.pad(row_module, REACH, constant_values=-1)
-    cols_pad = jnp.pad(col_module, REACH, constant_values=-1)
-    rows_near = lax.dynamic_slice_in_dim(rows_pad, row_start, tile_x + 2 * REACH, 0)
-    cols_near = lax.dynamic_slice_in_dim(cols_pad, col_start, tile_y + 2 * REACH, 0)
+        (tile_x + 2 * REACH, tile_y + 2 * REACH, 2 * hits + 2),
+    )
+    own = near[REACH : REACH + tile_x, REACH : REACH + tile_y, 2 * hits :]
     pieces = []
     for i in range(-REACH, REACH + 1):
         for j in range(-REACH, REACH + 1):
-            at_x, at_y = slice(REACH - i, REACH - i + tile_x), slice(REACH - j, REACH - j + tile_y)
-            row_same = rows_near[at_x] == rows_near[REACH : REACH + tile_x]
-            col_same = cols_near[at_y] == cols_near[REACH : REACH + tile_y]
-            allowed = row_same[:, None] & col_same[None, :]
-            pieces.append(jnp.where(allowed[..., None], near[at_x, at_y], -1.0))
+            piece = near[REACH - i : REACH - i + tile_x, REACH - j : REACH - j + tile_y]
+            allowed = jnp.all(piece[..., 2 * hits :] == own, axis=-1, keepdims=True)
+            pieces.append(jnp.where(allowed, piece[..., : 2 * hits], -1.0))
+    rows_pad = jnp.pad(row_module, REACH, constant_values=-1)
     sources = jnp.stack(pieces, 0).reshape(SPAN * SPAN, pixels, 2 * hits).transpose(0, 2, 1)
     sources = along_ticks(sources, hits)
 
@@ -272,10 +298,10 @@
             jax.ShapeDtypeStruct((over_y, pixels, reach), jnp.bfloat16),
         ],
         scratch_shapes=[
-            pltpu.VMEM((SPAN * SPAN * ROWS, SHIFTS * pixels), jnp.bfloat16),
-            pltpu.VMEM((SPAN * SPAN * ROWS, wave), jnp.bfloat16),
-        ],
-        compiler_params=pltpu.CompilerParams(vmem_limit_bytes=VMEM_BYTES),
+            pltpu.VMEM((SPAN * STACK, SHIFTS * pixels), jnp.bfloat16),
+            pltpu.VMEM((SPAN * STACK, wave), jnp.bfloat16),
+        ],
+        compiler_params=pltpu.CompilerParams(vmem_limit_bytes=60 * MIB),
         name="forward",
     )(
         sources,
@@ -284,7 +310,7 @@
         active.astype(jnp.float32).reshape(pixels, 1),
     )
 
-    everyone = everywhere(window, over_x, over_y, 1, "residuals")
+    everyone = everywhere(window, over_x, over_y, 1, 24, "residuals")
     everyone = everyone.reshape(over_x, over_y, tile_x, tile_y, reach)
     everyone = everyone.transpose(1, 3, 0, 2, 4).reshape(cols, rows, reach)
 
@@ -307,13 +333,13 @@
             ],
             out_specs=pl.BlockSpec((SPAN * SPAN, BINS, share), lambda y, c: (0, 0, 0)),
             scratch_shapes=[
-                pltpu.VMEM((REACH + 1, SPAN * ROWS, SHIFTS * rows), jnp.bfloat16),
+                pltpu.VMEM((REACH + 1, STACK, SHIFTS * rows), jnp.bfloat16),
                 pltpu.VMEM((REACH + 1, SHIFTS * rows, ticks_wide), jnp.bfloat16),
-                pltpu.VMEM((SPAN, SPAN * ROWS, ticks_wide), jnp.float32),
+                pltpu.VMEM((SPAN, STACK, ticks_wide), jnp.float32),
             ],
         ),
         out_shape=jax.ShapeDtypeStruct((SPAN * SPAN, BINS, share), jnp.float32),
-        compiler_params=pltpu.CompilerParams(vmem_limit_bytes=VMEM_BYTES),
+        compiler_params=pltpu.CompilerParams(vmem_limit_bytes=40 * MIB),
         name="backward",
     )(col_module, columns, row_mask, everyone)
     return current.reshape(tile_x, tile_y, wave), gradient

time: 61 us -> 65 us (1.066); the launches traced: 60.6 us -> 63.9 us
  local copies, waits for them, and re-layouts: 7.92 us -> 10.6 us
    pallas_call x1, Pallas kernels: 3.73 us -> 7.26 us  [on_device(): pl.pallas_call(functools.partial(forward_kernel, hits, pixels, share, ove...]
    pallas_call x1, Pallas kernels: 19.7 us -> 16.7 us  [on_device(): pl.pallas_call(functools.partial(backward_kernel, hits, 1.0 / pixels), gr...]
    select_n x0 -> x25, local copies, waits for them, and re-layouts: none -> 2.56 us  [on_device(): pieces.append(jnp.where(allowed, piece[..., :2 * hits], -1.0))]
    unnamed x28, local copies, waits for them, and re-layouts: 2.7 us -> 0.85 us
    dynamic_slice x2 -> x0, local copies, waits for them, and re-layouts: 1.47 us -> none  [the longest x1 0.74 us: on_device(): lax.dynamic_slice_in_dim(rows_pad, row_start, tile_x + 2 * REACH, 0)]
    another operation x0 -> x2, local copies, waits for them, and re-layouts: none -> 1.38 us  [on_device(): jnp.stack([jnp.broadcast_to(row_module[:, None], (rows, cols)), jnp.broad...]
    reduce_sum x1 -> x0, other arithmetic: 0.88 us -> none  [first_of(): total = jnp.sum(jnp.where(same, charge[..., None, :], 0.0), axis=-1)]
    concatenate x1 -> x2, other arithmetic: 0.08 us -> 0.94 us  [the longest x1 0.77 us: on_device(): jnp.concatenate([(hit_bins * SHIFTS + hit_ticks).astype(jnp.float32), cha...]
where the time goes in v2:
time: 65 us; the launch traced here: 63.9 us
  Pallas kernels  47.5 us (73%)
  local copies, waits for them, and re-layouts  10.6 us (16%)
  other arithmetic  4.88 us (8%)
  between operations  0.94 us (1%)
    pallas_call x2, Pallas kernels, everywhere(): pl.pallas_call(gather_kernel, in_specs=[pl.BlockSpec(memory_space=pltpu.V...  23.5 us
    pallas_call x1, Pallas kernels, on_device(): pl.pallas_call(functools.partial(backward_kernel, hits, 1.0 / pixels), gr...  16.7 us
    pallas_call x1, Pallas kernels, on_device(): pl.pallas_call(functools.partial(forward_kernel, hits, pixels, share, ove...  7.26 us
    select_n x25, local copies, waits for them, and re-layouts, on_device(): pieces.append(jnp.where(allowed, piece[..., :2 * hits], -1.0))  2.56 us
    reshape x1, local copies, waits for them, and re-layouts, on_device(): return (current.reshape(tile_x, tile_y, wave), gradient)  1.4 us
    reshape x1, local copies, waits for them, and re-layouts, on_device(): measured.reshape(pixels, wave)  1.39 us
    another operation x2, local copies, waits for them, and re-layouts, on_device(): jnp.stack([jnp.broadcast_to(row_module[:, None], (rows, cols)), jnp.broad...  1.38 us

profile of v2, /device:TPU:15, one launch (start us, length us, event | category | flops | bytes accessed | tf_op | source)
XLA Modules:
  0.0 63.9 jit_solution(16950198678403082517)
XLA Ops:
  0.7 0.1 sub.31
  0.7 0.7 %convert_element_type.20 = f32[4,4]{1,0:T(4,128)S(1)} convert(s32[4,4]{1,0:T(4,128)} %param.12) | non-fusion elementwise | flops 16 | bytes 128 | tf_op jit(solution)/shard_map/convert_element_type | solution.py:310
  1.4 0.9 %fusion.39 = (f32[1,64]{1,0:T(1,128)S(1)}, f32[1,64]{1,0:T(1,128)S(1)}, f32[1,64]{1,0:T(1,128)S(1)}, f32[1,64]{1,0:T(1,128)S(1)}) fusion(s32[64]{0:T(128)} %param.14), kind=kLoop, calls=%fused_computation.128 | loop fusion | flops 512 | bytes 1280 | tf_op jit(solution)/shard_map/stack | solution.py:321
  2.4 0.1 tile.10.mask_ref
  2.5 0.7 %stack_broadcast_in_dim.4 = s32[64,8,1]{0,1,2:T(8,128)S(1)} broadcast(s32[64]{0:T(128)} %param.14), dimensions={0} | broadcast | bytes 2304 | tf_op jit(solution)/shard_map/stack;broadcast_in_dim | solution.py:256
  3.1 0.7 %stack_broadcast_in_dim.5 = s32[64,8,1]{0,1,2:T(8,128)S(1)} broadcast(s32[8]{0:T(128)} %cols_ref.1), dimensions={1} | broadcast | bytes 2080 | tf_op jit(solution)/shard_map/stack;broadcast_in_dim | solution.py:256
  3.9 0.1 sub.27
  3.9 0.7 %reshape.130.active_ref = f32[16,1]{1,0:T(8,128)} reshape(f32[4,4]{1,0:T(4,128)S(1)} %convert_element_type.20) | data formatting | bytes 128 | tf_op jit(solution)/shard_map/reshape | solution.py:310
  4.6 0.7 %add_convert_fusion.1 = f32[4,4,8]{2,1,0:T(4,128)S(1)} fusion(s32[4,4,8]{2,1,0:T(4,128)} %param.11, s32[4,4,8]{2,1,0:T(4,128)} %param.10), kind=kLoop, calls=%fused_computation.71 | loop fusion | flops 384 | bytes 1536 | tf_op jit(solution)/shard_map/convert_element_type | solution.py:248
  5.3 0.8 %pad_maximum_fusion = f32[4,4,16]{2,1,0:T(4,128)S(1)} fusion(f32[4,4,8]{2,1,0:T(4,128)} %param.9, f32[4,4,8]{2,1,0:T(4,128)S(1)} %add_convert_fusion.1), kind=kLoop, calls=%fused_computation.69 | loop fusion | flops 256 | bytes 2048 | tf_op jit(solution)/shard_map/concatenate | solution.py:247
  6.1 0.1 reshape.118.source_ref
  6.2 9.4 %deposits.1 = f32[16,2,2,128]{3,2,1,0:T(2,128)S(1)} custom-call(f32[1,2,128]{2,1,0:T(2,128)S(1)} %reshape.118.source_ref), custom_call_target="tpu_custom_call" | custom-call | tf_op jit(solution)/shard_map/deposits/pallas_call | solution.py:126
  15.6 1.4 %reshape.121.measured_ref = bf16[16,1024]{1,0:T(8,128)(2,1)} reshape(bf16[4,4,1024]{2,1,0:T(4,128)(2,1)} %param.13) | data formatting | bytes 65536 | tf_op jit(solution)/shard_map/reshape | solution.py:309
  16.9 0.2 reshape.119
  17.2 0.1 copy.18
  17.4 0.2 fusion.2
  17.5 0.1 fusion.26
  17.6 0.1 fusion.35
  17.8 0.1 copy.46
  17.9 0.1 broadcast_in_dim.247
  18.0 0.1 broadcast_in_dim.248
  18.1 0.1 subtract_select_fusion.1.cc_ref
  18.2 0.2 slice_select_fusion.5
  18.4 0.1 copy.38
  18.5 0.1 copy.22
  18.6 0.1 copy.21
  18.7 0.1 copy.33
  18.8 0.1 copy.20
  18.9 0.1 copy.19
  19.0 0.1 copy.32
  19.1 0.2 slice_select_fusion
  19.3 0.1 copy.43
  19.4 0.1 copy.42
  19.5 0.1 copy.31
  19.6 0.1 copy.30
  19.7 0.1 copy.37
  19.8 0.1 copy.29
  19.9 0.1 copy.40
  20.0 0.1 copy.28
  20.1 0.1 copy.36
  20.2 0.2 slice_select_fusion.2
  20.4 0.1 copy.41
  20.5 0.1 copy.27
  20.6 0.1 copy.26
  20.7 0.1 copy.35
  20.8 0.1 copy.25
  20.9 0.1 copy.39
  21.0 0.1 copy.24
  21.1 0.1 copy.23
  21.3 0.1 copy.34
  21.5 0.1 copy.44
  21.6 0.2 broadcast_in_dim.244
  21.8 0.4 broadcast_in_dim.245
  22.3 0.8 %subtract_select_fusion.cc_ref = f32[25,16,128]{2,1,0:T(8,128)} fusion(f32[25,16,128]{2,1,0:T(8,128)S(1)} %broadcast_in_dim.245, f32[128]{0:T(128)S(1)} %sub.27, pred[16]{0:T(512)(128)(4,1)S(1)} %iota_compare_fusion), kind=kLoop, calls=%fused_computation.1 | loop fusion | flops 102400 | bytes 410128 | tf_op jit(solution)/shard_map/jit(_where)/select_n | solution.py:232
  23.1 7.3 %forward.1 = (bf16[16,1024]{1,0:T(8,128)(2,1)}, bf16[2,16,640]{2,1,0:T(8,128)(2,1)}) custom-call(f32[25,16,128]{2,1,0:T(8,128)} %subtract_select_fusion.cc_ref, f32[25,50,1000]{2,1,0:T(8,128)} %table_ref.1, bf16[16,1024]{1,0:T(8,128)(2,1)} %reshape.121.measured_ref, f32[16,1]{1,0:T(8,128)} %reshape.130.active_ref), custom_call_target="tpu_custom_call" | custom-call | tf_op jit(solution)/shard_map/forward/pallas_call | solution.py:283
  30.3 0.0 copy-start.1
  30.3 1.4 %reshape.123 = bf16[4,4,1024]{2,1,0:T(4,128)(2,1)} reshape(bf16[16,1024]{1,0:T(8,128)(2,1)} %get-tuple-element.4) | data formatting | bytes 65536 | tf_op jit(solution)/shard_map/reshape | solution.py:345
  31.7 0.8 %copy-done = bf16[2,16,640]{2,1,0:T(8,128)(2,1)S(1)} copy-done((bf16[2,16,640]{2,1,0:T(8,128)(2,1)S(1)}, bf16[2,16,640]{2,1,0:T(8,128)(2,1)}, u32[]{:S(2)}) %copy-start) | copy-done | bytes 40984
  32.5 14.1 %residuals.1 = bf16[16,2,16,640]{3,2,1,0:T(8,128)(2,1)S(1)} custom-call(bf16[2,16,640]{2,1,0:T(8,128)(2,1)S(1)} %copy-done), custom_call_target="tpu_custom_call" | custom-call | tf_op jit(solution)/shard_map/residuals/pallas_call | solution.py:126
  46.7 0.2 reshape.124
  46.8 0.3 copy.49
  47.1 0.1 reshape.125.resid_ref
  47.2 0.0 copy-done.1
  47.2 16.7 %backward.1 = f32[25,50,500]{2,1,0:T(8,128)} custom-call(s32[8]{0:T(128)S(1)} %copy-done.1, f32[8,16,128]{2,1,0:T(8,128)S(1)} %subtract_select_fusion.1.cc_ref, f32[8,128]{1,0:T(8,128)S(1)} %tile.10.mask_ref, bf16[8,64,640]{2,1,0:T(8,128)(2,1)S(1)} %reshape.125.resid_ref), custom_call_target="tpu_custom_call" | custom-call | tf_op jit(solution)/shard_map/backward/pallas_call | solution.py:324
  (35 shorter events, 0.2 us)
Async XLA Ops:
  30.3 16.9 %copy-start.1 = (s32[8]{0:T(128)S(1)}, s32[8]{0:T(128)}, u32[]{:S(2)}) copy-start(s32[8]{0:T(128)} %cols_ref.1) | copy-start | bytes 100
  31.7 0.8 %copy-start = (bf16[2,16,640]{2,1,0:T(8,128)(2,1)S(1)}, bf16[2,16,640]{2,1,0:T(8,128)(2,1)}, u32[]{:S(2)}) copy-start(bf16[2,16,640]{2,1,0:T(8,128)(2,1)} %get-tuple-element.5.source_ref) | copy-start | bytes 122884
